TPU v7x, 32 devices: a whole 2x2x4 slice. The times are simulated.
32 devices in a mesh: parts: 2 (over y), tm: 4 (over z), factor: 4 (over x, core).
Axes of the slice: x: 2, y: 2, z: 4, core: 2. Of those that a mesh axis runs over, the one named last changes fastest.
Arguments:
- schur_matrix: float32 [24576, 24, 4, 128], P(('parts', 'tm'), None, 'factor'), parts along dimension 0, as said below
- link_rhs: float32 [24576], P(('parts', 'tm')), parts along dimension 0, may hold values from -6 to 6
- hour_rhs: float32 [32, 256], P(('parts', 'tm', 'factor')), parts along dimension 0, may hold values from -6 to 6
- link_cols: int32 [32, 256], P(('parts', 'tm', 'factor')), parts along dimension 0, may hold values from 0 to 255
- link_coef: float32 [32, 256], P(('parts', 'tm', 'factor')), parts along dimension 0, may hold values from -6 to 6
- hour_inverse: float32 [32, 256, 256], P(('parts', 'tm', 'factor')), parts along dimension 0, may hold values from -0.375 to 0.375
- couple_prev: float32 [32, 2, 256], P(('parts', 'tm', 'factor')), parts along dimension 0, may hold values from -1.2 to 1.2
- couple_next: float32 [32, 2, 256], P(('parts', 'tm', 'factor')), parts along dimension 0, may hold values from -1.2 to 1.2
Outputs:
- schur_trail: float32 [24576, 24, 4, 128], P(('parts', 'tm'), None, 'factor'), parts along dimension 0
- link_trail: float32 [24576], P(('parts', 'tm')), parts along dimension 0
- hour_step: float32 [32, 256], P(('parts', 'tm', 'factor')), parts along dimension 0
There are 2 independent parts, one for each index of `parts`. A program takes and returns all parts, laid end to end along the dimension named above; each array names one. Nothing has to cross between parts.
Inputs may be any that keep to these rules, and one draw needn't show every extreme that they name: schur_matrix is symmetric and its leading 2 * 128 rows and columns form a positive definite block.
All inputs are finite; a program needn't handle non-finite values.
Results may differ from a plain program's by a relative error of at most 0.0001.
Values sent between devices are 32-bit elements; how exact they have to be, the bound alone decides.
A program may use at most 192 MiB of HBM per device.

v0:
```python
import jax
import jax.numpy as jnp
from jax import lax
from jax.sharding import PartitionSpec as P

PANELS = 2
BW = 2
SWEEPS = 2


def spread(array, axis, root):
    mine = lax.axis_index(axis) == root
    return lax.psum(jnp.where(mine, array, jnp.zeros_like(array)), axis)


def with_halo(cells, sides, width):
    for axis, dim in sides:
        count = lax.axis_size(axis)
        ends = count - 1
        head = lax.slice_in_dim(cells, 0, width, axis=dim)
        tail = lax.slice_in_dim(cells, cells.shape[dim] - width, cells.shape[dim], axis=dim)
        cells = jnp.concatenate(
            [
                lax.ppermute(tail, axis, [(i, (i + 1) % count) for i in range(ends)]),
                cells,
                lax.ppermute(head, axis, [((i + 1) % count, i) for i in range(ends)]),
            ],
            axis=dim,
        )
    return cells


def shards(
    schur_matrix, link_rhs, hour_rhs, link_cols, link_coef, hour_inverse, couple_prev, couple_next
):
    rows_here = schur_matrix.shape[0]
    tiles_here = schur_matrix.shape[1]
    width = schur_matrix.shape[3]
    factors = lax.axis_size("factor")
    row_start = lax.axis_index("tm") * rows_here
    global_rows = row_start + jnp.arange(rows_here, dtype=jnp.int32)
    factor_here = lax.axis_index("factor")
    schur_now = schur_matrix
    rhs_now = link_rhs
    solved = []
    for panel_id in range(PANELS):
        column_tile = panel_id // factors
        owner_index = panel_id % factors
        own_cols = schur_now[:, column_tile, 0, :]
        panel_cols = spread(own_cols, "factor", owner_index)
        panel_first = panel_id * width
        picker = (
            global_rows[:, None] - panel_first == jnp.arange(width, dtype=jnp.int32)[None, :]
        ).astype(jnp.float32)
        block_part = jnp.dot(picker.T, panel_cols, precision=lax.Precision.HIGHEST)
        rhs_part = jnp.dot(picker.T, rhs_now, precision=lax.Precision.HIGHEST)
        diag_block, rhs_segment = lax.psum((block_part, rhs_part), "tm")
        lower_block = jnp.linalg.cholesky(diag_block)
        factor_rows = jax.scipy.linalg.solve_triangular(lower_block, panel_cols.T, lower=True).T
        factor_rows = jnp.where(
            (global_rows < panel_first)[:, None], jnp.zeros_like(factor_rows), factor_rows
        )
        all_factor = lax.all_gather(factor_rows, "tm", axis=0, tiled=True)
        grouped = all_factor.reshape(tiles_here, factors, width, width)
        my_tiles = lax.dynamic_index_in_dim(grouped, factor_here, 1, keepdims=False)
        link_step = jax.scipy.linalg.solve_triangular(lower_block, rhs_segment, lower=True)
        rhs_now = rhs_now - jnp.dot(factor_rows, link_step, precision=lax.Precision.HIGHEST)
        update = jnp.einsum("rk,tck->rtc", factor_rows, my_tiles, precision=lax.Precision.HIGHEST)
        schur_now = schur_now - update[:, :, None, :]
        solved.append(link_step)
    link_values = jnp.concatenate(solved)
    one_hot = (
        link_cols[:, :, None] == jnp.arange(PANELS * width, dtype=jnp.int32)[None, None, :]
    ).astype(jnp.float32)
    looked = jnp.einsum("hik,k->hi", one_hot, link_values, precision=lax.Precision.HIGHEST)
    target = hour_rhs - link_coef * looked
    hour_state = jnp.einsum("hik,hk->hi", hour_inverse, target, precision=lax.Precision.HIGHEST)
    for sweep_id in range(SWEEPS):
        border_pairs = jnp.concatenate((hour_state[:, :BW], hour_state[:, -BW:]), axis=1)
        padded = with_halo(border_pairs, ((("tm", "factor"), 0),), 1)
        prev_last = padded[:-2, BW:]
        next_first = padded[2:, :BW]
        coupling = jnp.einsum("hbi,hb->hi", couple_prev, prev_last, precision=lax.Precision.HIGHEST)
        coupling = coupling + jnp.einsum(
            "hbi,hb->hi", couple_next, next_first, precision=lax.Precision.HIGHEST
        )
        hour_state = jnp.einsum(
            "hik,hk->hi", hour_inverse, target - coupling, precision=lax.Precision.HIGHEST
        )
    return (schur_now, rhs_now, hour_state)


def solution(mesh):
    placed = (
        P(("parts", "tm"), None, "factor", None),
        P(("parts", "tm")),
        P(("parts", "tm", "factor"), None),
        P(("parts", "tm", "factor"), None),
        P(("parts", "tm", "factor"), None),
        P(("parts", "tm", "factor"), None, None),
        P(("parts", "tm", "factor"), None, None),
        P(("parts", "tm", "factor"), None, None),
    )
    return jax.shard_map(
        shards,
        mesh=mesh,
        in_specs=placed,
        out_specs=(
            P(("parts", "tm"), None, "factor", None),
            P(("parts", "tm")),
            P(("parts", "tm", "factor"), None),
        ),
        check_vma=False,
    )
```

profile of v0, /device:TPU:0, one launch (start us, length us, event | category | flops | bytes accessed | tf_op | source)
XLA Modules:
  0.0 661.5 jit_solution(964721345408237185)
XLA Ops:
  7.2 32.9 %copy.16 = f32[3072,24,1,128]{3,0,1,2:T(8,128)} copy(f32[3072,24,1,128]{3,2,1,0:T(1,128)} %param.13) | data formatting | bytes 75497472 | tf_op args[0]
  42.9 45.6 %all-reduce.5.cloned.1.call-done = f32[3072,128]{1,0:T(8,128)} async-done(((f32[3072,128]{1,0:T(8,128)}), f32[3072,128]{1,0:T(8,128)}) %all-reduce.5.cloned.1.call-update) | async-done | bytes 1572880 | tf_op jit(solution)/shard_map/psum | solution.py:13
  88.6 4.0 fusion.8
  92.6 34.1 %all-reduce.7.cloned.1.call-done = f32[128,128]{0,1:T(8,128)} async-done(((f32[128,128]{0,1:T(8,128)}), f32[128,128]{0,1:T(8,128)}) %all-reduce.7.cloned.1.call-update) | async-done | bytes 65552 | tf_op jit(solution)/shard_map/psum | solution.py:57
  128.6 11.7 %cholesky.44 = f32[128,128]{1,0:T(8,128)S(1)} custom-call(f32[128,128]{1,0:T(8,128)S(1)} %fusion.35), custom_call_target="Cholesky" | custom-call | tf_op jit(solution)/shard_map/jit(cholesky)/cholesky | solution.py:58
  141.6 9.8 %custom-call.10 = f32[1,128,128]{1,2,0:T(8,128)S(1)} custom-call(f32[1,128,128]{2,1,0:T(8,128)S(1)} %fusion.26), custom_call_target="InvertDiagBlocksLowerTriangular" | custom-call | tf_op jit(solution)/shard_map/jit(_solve_triangular)/triangular_solve | solution.py:59
  154.7 114.7 %all-gather.3.cloned.1.call-done = f32[12288,128]{0,1:T(8,128)} async-done(((f32[3072,128]{0,1:T(8,128)}), f32[12288,128]{0,1:T(8,128)}) %all-gather.3.cloned.1.call-update) | async-done | bytes 6291472 | tf_op jit(solution)/shard_map/all_gather | solution.py:63
  269.3 8.3 %reshape.109 = f32[24,4,128,128]{2,1,0,3:T(4,128)} reshape(f32[12288,128]{0,1:T(8,128)} %all-gather.3.cloned.1.call-done) | data formatting | bytes 12582912 | tf_op jit(solution)/shard_map/reshape | solution.py:64
  277.7 5.6 constant_dynamic-slice_fusion.1
  283.2 3.8 copy.14
  287.1 41.2 %bitcast_subtract_fusion.1 = f32[3072,24,1,128]{3,0,1,2:T(8,128)} fusion(f32[24,1,128,128]{3,2,0,1:T(8,128)S(1)} %copy.14, f32[128,3072]{1,0:T(8,128)S(1)} %copy-done.3, f32[3072,24,1,128]{3,2,1,0:T(1,128)} %param.13), kind=kOutput, calls=%fused_computation.1 | convolution fusion | flops 14504951808 | bytes 78643200 | tf_op jit(solution)/shard_map/rk,tck->rtc/dot_general | solution.py:68
  331.1 41.1 %all-reduce.9.cloned.1.call-done = f32[3072,128]{1,0:T(8,128)} async-done(((f32[3072,128]{1,0:T(8,128)}), f32[3072,128]{1,0:T(8,128)}) %all-reduce.9.cloned.1.call-update) | async-done | bytes 1572880 | tf_op jit(solution)/shard_map/psum | solution.py:13
  372.2 4.0 fusion.9
  376.5 34.0 %all-reduce.11.cloned.1.call-done = f32[128,128]{0,1:T(8,128)} async-done(((f32[128,128]{0,1:T(8,128)}), f32[128,128]{0,1:T(8,128)}) %all-reduce.11.cloned.1.call-update) | async-done | bytes 65552 | tf_op jit(solution)/shard_map/psum | solution.py:57
  412.9 12.5 %cholesky.55 = f32[128,128]{1,0:T(8,128)S(1)} custom-call(f32[128,128]{1,0:T(8,128)} %fusion.31), custom_call_target="Cholesky" | custom-call | tf_op jit(solution)/shard_map/jit(cholesky)/cholesky | solution.py:58
  427.4 10.6 %custom-call.11 = f32[1,128,128]{1,2,0:T(8,128)S(1)} custom-call(f32[1,128,128]{2,1,0:T(8,128)} %fusion.27), custom_call_target="InvertDiagBlocksLowerTriangular" | custom-call | tf_op jit(solution)/shard_map/jit(_solve_triangular)/triangular_solve | solution.py:59
  442.9 10.7 %psum.46 = f32[128]{0:T(128)S(1)} all-reduce(f32[128]{0:T(128)} %fusion.14), channel_id=1, replica_groups=mesh['parts'=2,'tm'=4,'factor'=4] {'tm'}, use_global_device_ids=true, to_apply=%region_6.9 | all-reduce | flops 128 | bytes 1024 | tf_op jit(solution)/shard_map/psum | solution.py:57
  456.9 8.7 %psum.47 = f32[128]{0:T(128)S(1)} all-reduce(f32[128]{0:T(128)S(1)} %fusion.13), channel_id=1, replica_groups=mesh['parts'=2,'tm'=4,'factor'=4] {'tm'}, use_global_device_ids=true, to_apply=%region_7.11 | all-reduce | flops 128 | bytes 1024 | tf_op jit(solution)/shard_map/psum | solution.py:57
  475.3 3.9 collective-permute-start.2
  480.9 75.3 %all-gather.5.cloned.1.call-done = f32[12288,128]{0,1:T(8,128)} async-done(((f32[3072,128]{0,1:T(8,128)}), f32[12288,128]{0,1:T(8,128)}) %all-gather.5.cloned.1.call-update) | async-done | bytes 6291472 | tf_op jit(solution)/shard_map/all_gather | solution.py:63
  556.2 8.3 %reshape.110 = f32[24,4,128,128]{2,1,0,3:T(4,128)} reshape(f32[12288,128]{0,1:T(8,128)} %all-gather.5.cloned.1.call-done) | data formatting | bytes 12582912 | tf_op jit(solution)/shard_map/reshape | solution.py:64
  564.5 5.6 constant_dynamic-slice_fusion
  573.8 37.3 %bitcast_subtract_fusion = f32[3072,24,1,128]{3,0,1,2:T(8,128)} fusion(f32[3072,24,1,128]{3,0,1,2:T(8,128)} %bitcast_subtract_fusion.1, f32[24,1,128,128]{3,2,0,1:T(8,128)S(1)} %copy.19, f32[128,3072]{1,0:T(8,128)S(1)} %copy-done.2), kind=kOutput, calls=%fused_computation | convolution fusion | flops 14504951808 | bytes 78643200 | tf_op jit(solution)/shard_map/rk,tck->rtc/dot_general | solution.py:68
  611.1 43.3 %copy.21 = f32[3072,24,1,128]{3,2,1,0:T(1,128)} copy(f32[3072,24,1,128]{3,0,1,2:T(8,128)} %bitcast_subtract_fusion) | data formatting | bytes 75497472
  (81 shorter events, 39.6 us)
Async XLA Ops:
  7.2 459.6 %copy-start = (f32[1,256,256]{2,1,0:T(8,128)S(1)}, f32[1,256,256]{2,1,0:T(8,128)}, u32[]{:S(2)}) copy-start(f32[1,256,256]{2,1,0:T(8,128)} %param.18) | copy-start | bytes 786436
  7.2 81.4 %all-reduce.5.cloned.1.call-start = ((), (), s32[]{:S(2)}) async-start(), calls=%async_computation | async-start | bytes 3145728 | tf_op jit(solution)/shard_map/psum | solution.py:13
  42.9 83.9 %all-reduce.7.cloned.1.call-start = ((), (), s32[]{:S(2)}) async-start(), calls=%async_computation.1 | async-start | bytes 131072 | tf_op jit(solution)/shard_map/psum | solution.py:57
  88.6 62.9 %copy-start.4 = (f32[3072,128]{1,0:T(8,128)S(1)}, f32[3072,128]{1,0:T(8,128)}, u32[]{:S(2)}) copy-start(f32[3072,128]{1,0:T(8,128)} %all-reduce.5.cloned.1.call-done) | copy-start | bytes 4718596
  92.6 176.8 %all-gather.3.cloned.1.call-start = ((), (), s32[]{:S(2)}) async-start(), calls=%async_computation.2 | async-start | bytes 7864320 | tf_op jit(solution)/shard_map/all_gather | solution.py:63
  154.1 218.1 %all-reduce.9.cloned.1.call-start = ((), (), s32[]{:S(2)}) async-start(), calls=%async_computation.3 | async-start | bytes 3145728 | tf_op jit(solution)/shard_map/psum | solution.py:13
  283.2 3.9 copy-start.3
  331.0 79.4 %all-reduce.11.cloned.1.call-start = ((), (), s32[]{:S(2)}) async-start(), calls=%async_computation.4 | async-start | bytes 131072 | tf_op jit(solution)/shard_map/psum | solution.py:57
  331.1 45.4 %copy-start.6 = (s32[3072]{0:T(1024)}, s32[3072]{0:T(1024)S(1)}, u32[]{:S(2)}) copy-start(s32[3072]{0:T(1024)S(1)} %fusion.36) | copy-start | bytes 36868
  372.2 65.8 %copy-start.5 = (f32[3072,128]{1,0:T(8,128)S(1)}, f32[3072,128]{1,0:T(8,128)}, u32[]{:S(2)}) copy-start(f32[3072,128]{1,0:T(8,128)} %all-reduce.9.cloned.1.call-done) | copy-start | bytes 4718596
  376.2 180.0 %all-gather.5.cloned.1.call-start = ((), (), s32[]{:S(2)}) async-start(), calls=%async_computation.5 | async-start | bytes 7864320 | tf_op jit(solution)/shard_map/all_gather | solution.py:63
  440.7 25.0 %copy-start.9 = (f32[1,256]{1,0:T(1,128)S(1)}, f32[1,256]{1,0:T(1,128)}, u32[]{:S(2)}) copy-start(f32[1,256]{1,0:T(1,128)} %param.15) | copy-start | bytes 3076
  440.7 30.9 %copy-start.2 = (f32[128,3072]{1,0:T(8,128)S(1)}, f32[128,3072]{1,0:T(8,128)}, u32[]{:S(2)}) copy-start(f32[128,3072]{1,0:T(8,128)} %convolution_select_fusion) | copy-start | bytes 4718596
  454.7 18.5 %copy-start.7 = (f32[1,2,256]{2,1,0:T(2,128)S(1)}, f32[1,2,256]{2,1,0:T(2,128)}, u32[]{:S(2)}) copy-start(f32[1,2,256]{2,1,0:T(2,128)} %param.20) | copy-start | bytes 6148
  454.7 18.6 %copy-start.8 = (f32[1,2,256]{2,1,0:T(2,128)S(1)}, f32[1,2,256]{2,1,0:T(2,128)}, u32[]{:S(2)}) copy-start(f32[1,2,256]{2,1,0:T(2,128)} %param.19) | copy-start | bytes 6148
  467.3 5.9 collective-permute-start.1
  468.6 4.7 collective-permute-start
  474.0 5.2 collective-permute-start.3
  475.3 4.5 collective-permute-start.2
  611.1 43.3 %copy-start.1 = (f32[1,256,256]{2,1,0:T(8,128)S(1)}, f32[1,256,256]{2,1,0:T(8,128)}, u32[]{:S(2)}) copy-start(f32[1,256,256]{2,1,0:T(8,128)} %param.18) | copy-start | bytes 786436
Sparse Core Ops, SparseCore 0:
  43.0 45.5 all-reduce.4
  92.7 34.0 all-reduce.6
  154.3 115.0 all-gather.2
  331.1 41.0 all-reduce.8
  376.4 34.0 all-reduce.10
  440.8 115.3 all-gather.4
where the time goes:
time: 671 us; the launch traced here: 662 us
  waiting for transfers between devices  345 us (51%)
  local copies, waits for them, and re-layouts  114 us (17%)
  matrix products  101 us (15%)
  other arithmetic  57.2 us (9%)
  blocking collectives  19.4 us (3%)
  between operations  14.7 us (2%)
  starting transfers between devices  10.4 us (2%)
    all_gather x2, waiting for transfers between devices, shards(): all_factor = lax.all_gather(factor_rows, 'tm', axis=0, tiled=True)  190 us
    psum x2, waiting for transfers between devices, spread(): return lax.psum(jnp.where(mine, array, jnp.zeros_like(array)), axis)  86.8 us
    dot_general x2, matrix products, shards(): jnp.einsum('rk,tck->rtc', factor_rows, my_tiles, precision=lax.Precision....  78.5 us
    unnamed x22, local copies, waits for them, and re-layouts  76.3 us
    psum x2, waiting for transfers between devices, shards(): diag_block, rhs_segment = lax.psum((block_part, rhs_part), 'tm')  68.1 us
    another operation x6, other arithmetic, shards(): lower_block = jnp.linalg.cholesky(diag_block)  25.6 us
    another operation x4, other arithmetic, shards(): jax.scipy.linalg.solve_triangular(lower_block, panel_cols.T, lower=True)  22.4 us
    psum x2, blocking collectives, shards(): diag_block, rhs_segment = lax.psum((block_part, rhs_part), 'tm')  19.4 us
  transfers between devices with their start and end apart: 10, of which 7 were waited for; matrix products, arithmetic and copies ran while one was open for 2% of the time, Pallas kernels for 0%

commit v1 on v0

--- a/solution.py
+++ b/solution.py
@@ -6,6 +6,24 @@
 PANELS = 2
 BW = 2
 SWEEPS = 2
+
+
+def gather_around(shard, axis, dim):
+    ways, here, step = (lax.axis_size(axis), lax.axis_index(axis), shard.shape[dim])
+    lengths = [n * ways if d == dim else n for d, n in enumerate(shard.shape)]
+    full = lax.dynamic_update_slice_in_dim(
+        jnp.zeros(lengths, shard.dtype), shard, here * step, axis=dim
+    )
+    going_up = going_down = shard
+    for far in range(1, ways // 2 + 1):
+        going_up = lax.ppermute(going_up, axis, [(d, (d + 1) % ways) for d in range(ways)])
+        full = lax.dynamic_update_slice_in_dim(full, going_up, (here - far) % ways * step, axis=dim)
+        if 2 * far < ways:
+            going_down = lax.ppermute(going_down, axis, [(d, (d - 1) % ways) for d in range(ways)])
+            full = lax.dynamic_update_slice_in_dim(
+                full, going_down, (here + far) % ways * step, axis=dim
+            )
+    return full
 
 
 def spread(array, axis, root):
@@ -60,7 +78,7 @@
         factor_rows = jnp.where(
             (global_rows < panel_first)[:, None], jnp.zeros_like(factor_rows), factor_rows
         )
-        all_factor = lax.all_gather(factor_rows, "tm", axis=0, tiled=True)
+        all_factor = gather_around(factor_rows, "tm", 0)
         grouped = all_factor.reshape(tiles_here, factors, width, width)
         my_tiles = lax.dynamic_index_in_dim(grouped, factor_here, 1, keepdims=False)
         link_step = jax.scipy.linalg.solve_triangular(lower_block, rhs_segment, lower=True)

time: 671 us -> 625 us (0.931)
  the two profiles are of different devices: /device:TPU:0 before, /device:TPU:16 now
where the time goes in v1:
time: 625 us; the launch traced here: 616 us
  waiting for transfers between devices  308 us (49%)
  local copies, waits for them, and re-layouts  108 us (17%)
  matrix products  102 us (16%)
  other arithmetic  53.6 us (9%)
  blocking collectives  17.4 us (3%)
  between operations  14.3 us (2%)
  starting transfers between devices  13.7 us (2%)
    ppermute x4, waiting for transfers between devices, gather_around(): lax.ppermute(going_up, axis, [(d, (d + 1) % ways) for d in range(ways)])  122 us
    dot_general x2, matrix products, shards(): jnp.einsum('rk,tck->rtc', factor_rows, my_tiles, precision=lax.Precision....  84.6 us
    unnamed x28, local copies, waits for them, and re-layouts  78.9 us
    psum x2, waiting for transfers between devices, spread(): return lax.psum(jnp.where(mine, array, jnp.zeros_like(array)), axis)  76.1 us
    psum x2, waiting for transfers between devices, shards(): diag_block, rhs_segment = lax.psum((block_part, rhs_part), 'tm')  58.1 us
    ppermute x2, waiting for transfers between devices, with_halo(): lax.ppermute(tail, axis, [(i, (i + 1) % count) for i in range(ends)])  51.6 us
    another operation x6, other arithmetic, shards(): lower_block = jnp.linalg.cholesky(diag_block)  24.8 us
    another operation x4, other arithmetic, shards(): jax.scipy.linalg.solve_triangular(lower_block, panel_cols.T, lower=True)  20.9 us
  transfers between devices with their start and end apart: 14, of which 9 were waited for; matrix products, arithmetic and copies ran while one was open for 4% of the time, Pallas kernels for 0%

profile of v1, /device:TPU:16, one launch (start us, length us, event | category | flops | bytes accessed | tf_op | source)
XLA Modules:
  0.0 616.0 jit_solution(1532008256796375847)
XLA Ops:
  7.2 32.9 %copy.28 = f32[3072,24,1,128]{3,0,1,2:T(8,128)} copy(f32[3072,24,1,128]{3,2,1,0:T(1,128)} %param.13) | data formatting | bytes 75497472 | tf_op args[0]
  42.9 44.0 %all-reduce.5.cloned.1.call-done = f32[3072,128]{1,0:T(8,128)} async-done(((f32[3072,128]{1,0:T(8,128)}), f32[3072,128]{1,0:T(8,128)}) %all-reduce.5.cloned.1.call-update) | async-done | bytes 1572880 | tf_op jit(solution)/shard_map/psum | solution.py:31
  86.9 4.0 fusion.10
  91.0 33.9 %all-reduce.7.cloned.1.call-done = f32[128,128]{0,1:T(8,128)} async-done(((f32[128,128]{0,1:T(8,128)}), f32[128,128]{0,1:T(8,128)}) %all-reduce.7.cloned.1.call-update) | async-done | bytes 65552 | tf_op jit(solution)/shard_map/psum | solution.py:75
  126.7 11.7 %cholesky.44 = f32[128,128]{1,0:T(8,128)S(1)} custom-call(f32[128,128]{1,0:T(8,128)S(1)} %fusion.37), custom_call_target="Cholesky" | custom-call | tf_op jit(solution)/shard_map/jit(cholesky)/cholesky | solution.py:76
  139.7 9.8 %custom-call.10 = f32[1,128,128]{1,2,0:T(8,128)S(1)} custom-call(f32[1,128,128]{2,1,0:T(8,128)S(1)} %fusion.28), custom_call_target="InvertDiagBlocksLowerTriangular" | custom-call | tf_op jit(solution)/shard_map/jit(_solve_triangular)/triangular_solve | solution.py:77
  153.6 65.3 %collective-permute-done = f32[3072,128]{0,1:T(8,128)} collective-permute-done((f32[3072,128]{0,1:T(8,128)S(1)}, f32[3072,128]{0,1:T(8,128)}, u32[]{:S(2)}, u32[]{:S(2)}) %collective-permute-start) | collective-permute-done | bytes 1572896 | tf_op jit(solution)/shard_map/ppermute | solution.py:19
  219.3 2.9 broadcast.115.clone
  225.3 3.0 copy.25
  231.6 21.3 %collective-permute-done.2 = f32[3072,128]{0,1:T(8,128)} collective-permute-done((f32[3072,128]{0,1:T(8,128)}, f32[3072,128]{0,1:T(8,128)}, u32[]{:S(2)}, u32[]{:S(2)}) %collective-permute-start.2) | collective-permute-done | bytes 1572896 | tf_op jit(solution)/shard_map/ppermute | solution.py:19
  256.0 46.5 %bitcast_subtract_fusion.1 = f32[3072,24,1,128]{3,0,1,2:T(8,128)} fusion(f32[128,3072]{1,0:T(8,128)S(1)} %convolution_select_fusion.1, f32[24,4,128,128]{3,2,1,0:T(8,128)} %bitcast.7, s32[]{:T(128)S(6)} %select_n.90, f32[3072,24,1,128]{3,2,1,0:T(1,128)} %param.13), kind=kOutput, calls=%fused_computation.1 | convolution fusion | flops 14504951808 | bytes 78643200 | tf_op jit(solution)/shard_map/rk,tck->rtc/dot_general | solution.py:86
  306.7 8.5 %psum.46 = f32[128]{0:T(128)S(1)} all-reduce(f32[128]{0:T(128)S(1)} %fusion.16), channel_id=1, replica_groups=mesh['parts'=2,'tm'=4,'factor'=4] {'tm'}, use_global_device_ids=true, to_apply=%region_6.9 | all-reduce | flops 128 | bytes 1024 | tf_op jit(solution)/shard_map/psum | solution.py:75
  316.3 32.1 %all-reduce.9.cloned.1.call-done = f32[3072,128]{1,0:T(8,128)} async-done(((f32[3072,128]{1,0:T(8,128)}), f32[3072,128]{1,0:T(8,128)}) %all-reduce.9.cloned.1.call-update) | async-done | bytes 1572880 | tf_op jit(solution)/shard_map/psum | solution.py:31
  348.4 4.0 fusion.11
  353.2 8.9 %psum.47 = f32[128]{0:T(128)S(1)} all-reduce(f32[128]{0:T(128)S(1)} %fusion.15), channel_id=1, replica_groups=mesh['parts'=2,'tm'=4,'factor'=4] {'tm'}, use_global_device_ids=true, to_apply=%region_7.11 | all-reduce | flops 128 | bytes 1024 | tf_op jit(solution)/shard_map/psum | solution.py:75
  362.1 24.2 %all-reduce.11.cloned.1.call-done = f32[128,128]{0,1:T(8,128)} async-done(((f32[128,128]{0,1:T(8,128)}), f32[128,128]{0,1:T(8,128)}) %all-reduce.11.cloned.1.call-update) | async-done | bytes 65552 | tf_op jit(solution)/shard_map/psum | solution.py:75
  388.1 11.7 %cholesky.55 = f32[128,128]{1,0:T(8,128)S(1)} custom-call(f32[128,128]{1,0:T(8,128)S(1)} %fusion.33), custom_call_target="Cholesky" | custom-call | tf_op jit(solution)/shard_map/jit(cholesky)/cholesky | solution.py:76
  401.2 9.8 %custom-call.11 = f32[1,128,128]{1,2,0:T(8,128)S(1)} custom-call(f32[1,128,128]{2,1,0:T(8,128)S(1)} %fusion.29), custom_call_target="InvertDiagBlocksLowerTriangular" | custom-call | tf_op jit(solution)/shard_map/jit(_solve_triangular)/triangular_solve | solution.py:77
  423.5 21.3 %collective-permute-done.6 = f32[1,4]{1,0:T(1,128)S(1)} collective-permute-done((f32[1,4]{1,0:T(1,128)S(1)}, f32[1,4]{1,0:T(1,128)S(1)}, u32[]{:S(2)}, u32[]{:S(2)}) %collective-permute-start.6) | collective-permute-done | bytes 48 | tf_op jit(solution)/shard_map/ppermute | solution.py:42
  445.3 35.2 %collective-permute-done.3 = f32[3072,128]{0,1:T(8,128)} collective-permute-done((f32[3072,128]{0,1:T(8,128)S(1)}, f32[3072,128]{0,1:T(8,128)}, u32[]{:S(2)}, u32[]{:S(2)}) %collective-permute-start.3) | collective-permute-done | bytes 1572896 | tf_op jit(solution)/shard_map/ppermute | solution.py:19
  485.1 30.2 %collective-permute-done.8 = f32[1,4]{1,0:T(1,128)S(1)} collective-permute-done((f32[1,4]{1,0:T(1,128)S(1)}, f32[1,4]{1,0:T(1,128)S(1)}, u32[]{:S(2)}, u32[]{:S(2)}) %collective-permute-start.8) | collective-permute-done | bytes 48 | tf_op jit(solution)/shard_map/ppermute | solution.py:42
  518.4 3.0 copy.33
  527.8 38.1 %bitcast_subtract_fusion = f32[3072,24,1,128]{3,0,1,2:T(8,128)} fusion(f32[3072,24,1,128]{3,0,1,2:T(8,128)} %bitcast_subtract_fusion.1, f32[128,3072]{1,0:T(8,128)S(1)} %convolution_select_fusion, f32[24,4,128,128]{3,2,1,0:T(8,128)} %bitcast.150, s32[]{:T(128)S(6)} %select_n.90), kind=kOutput, calls=%fused_computation | convolution fusion | flops 14504951808 | bytes 78643200 | tf_op jit(solution)/shard_map/rk,tck->rtc/dot_general | solution.py:86
  566.0 43.3 %copy.36 = f32[3072,24,1,128]{3,2,1,0:T(1,128)} copy(f32[3072,24,1,128]{3,0,1,2:T(8,128)} %bitcast_subtract_fusion) | data formatting | bytes 75497472
  (105 shorter events, 55.9 us)
Async XLA Ops:
  7.2 406.5 %copy-start = (f32[1,256,256]{2,1,0:T(8,128)S(1)}, f32[1,256,256]{2,1,0:T(8,128)}, u32[]{:S(2)}) copy-start(f32[1,256,256]{2,1,0:T(8,128)} %param.18) | copy-start | bytes 786436
  7.2 79.7 %all-reduce.5.cloned.1.call-start = ((), (), s32[]{:S(2)}) async-start(), calls=%async_computation | async-start | bytes 3145728 | tf_op jit(solution)/shard_map/psum | solution.py:31
  42.9 82.0 %all-reduce.7.cloned.1.call-start = ((), (), s32[]{:S(2)}) async-start(), calls=%async_computation.1 | async-start | bytes 131072 | tf_op jit(solution)/shard_map/psum | solution.py:75
  86.9 62.6 %copy-start.4 = (f32[3072,128]{1,0:T(8,128)S(1)}, f32[3072,128]{1,0:T(8,128)}, u32[]{:S(2)}) copy-start(f32[3072,128]{1,0:T(8,128)} %all-reduce.5.cloned.1.call-done) | copy-start | bytes 4718596
  91.0 257.4 %all-reduce.9.cloned.1.call-start = ((), (), s32[]{:S(2)}) async-start(), calls=%async_computation.2 | async-start | bytes 3145728 | tf_op jit(solution)/shard_map/psum | solution.py:31
  151.1 67.8 %collective-permute-start = (f32[3072,128]{0,1:T(8,128)S(1)}, f32[3072,128]{0,1:T(8,128)}, u32[]{:S(2)}, u32[]{:S(2)}) collective-permute-start(f32[3072,128]{0,1:T(8,128)S(1)} %bitcast.144), channel_id=1, source_target_pairs={{0,4},{4,8},{8,12},{12,0},{1,5},{5,9},{9,13},{13,1},{2,6},{6,10},{... | collective-permute-start | bytes 4718600 | tf_op jit(solution)/shard_map/ppermute | solution.py:19
  151.7 73.7 %collective-permute-start.1 = (f32[3072,128]{0,1:T(8,128)S(1)}, f32[3072,128]{0,1:T(8,128)}, u32[]{:S(2)}, u32[]{:S(2)}) collective-permute-start(f32[3072,128]{0,1:T(8,128)S(1)} %bitcast.145), channel_id=1, source_target_pairs={{0,12},{4,0},{8,4},{12,8},{1,13},{5,1},{9,5},{13,9},{2,14},{6,2},{... | collective-permute-start | bytes 4718600 | tf_op jit(solution)/shard_map/ppermute | solution.py:22
  218.9 34.0 %collective-permute-start.2 = (f32[3072,128]{0,1:T(8,128)}, f32[3072,128]{0,1:T(8,128)}, u32[]{:S(2)}, u32[]{:S(2)}) collective-permute-start(f32[3072,128]{0,1:T(8,128)} %collective-permute-done), channel_id=1, source_target_pairs={{0,4},{4,8},{8,12},{12,0},{1,5},{5,9},{9,13},{13,1},{2,6},{6,10},{... | collective-permute-start | bytes 4718600 | tf_op jit(solution)/shard_map/ppermute | solution.py:19
  228.4 2.0 copy-start.6
  305.2 81.2 %all-reduce.11.cloned.1.call-start = ((), (), s32[]{:S(2)}) async-start(), calls=%async_computation.3 | async-start | bytes 131072 | tf_op jit(solution)/shard_map/psum | solution.py:75
  348.4 62.8 %copy-start.3 = (f32[3072,128]{1,0:T(8,128)S(1)}, f32[3072,128]{1,0:T(8,128)}, u32[]{:S(2)}) copy-start(f32[3072,128]{1,0:T(8,128)} %all-reduce.9.cloned.1.call-done) | copy-start | bytes 4718596
  411.2 2.2 copy-start.10
  411.2 2.2 copy-start.11
  411.2 2.2 copy-start.12
  412.7 67.8 %collective-permute-start.3 = (f32[3072,128]{0,1:T(8,128)S(1)}, f32[3072,128]{0,1:T(8,128)}, u32[]{:S(2)}, u32[]{:S(2)}) collective-permute-start(f32[3072,128]{0,1:T(8,128)S(1)} %bitcast.147), channel_id=1, source_target_pairs={{0,4},{4,8},{8,12},{12,0},{1,5},{5,9},{9,13},{13,1},{2,6},{6,10},{... | collective-permute-start | bytes 4718600 | tf_op jit(solution)/shard_map/ppermute | solution.py:19
  414.2 8.7 %collective-permute-start.7 = (f32[1,4]{1,0:T(1,128)S(1)}, f32[1,4]{1,0:T(1,128)S(1)}, u32[]{:S(2)}, u32[]{:S(2)}) collective-permute-start(f32[1,4]{1,0:T(1,128)S(1)} %pad_maximum_fusion.1), channel_id=1, source_target_pairs={{1,0},{2,1},{3,2},{4,3},{5,4},{6,5},{7,6},{8,7},{9,8},{10,9},{11,1... | collective-permute-start | bytes 56 | tf_op jit(solution)/shard_map/ppermute | solution.py:44
  416.1 28.7 %collective-permute-start.6 = (f32[1,4]{1,0:T(1,128)S(1)}, f32[1,4]{1,0:T(1,128)S(1)}, u32[]{:S(2)}, u32[]{:S(2)}) collective-permute-start(f32[1,4]{1,0:T(1,128)S(1)} %pad_maximum_fusion.1), channel_id=1, source_target_pairs={{0,1},{1,2},{2,3},{3,4},{4,5},{5,6},{6,7},{7,8},{8,9},{9,10},{10,1... | collective-permute-start | bytes 56 | tf_op jit(solution)/shard_map/ppermute | solution.py:42
  419.0 99.4 %collective-permute-start.4 = (f32[3072,128]{0,1:T(8,128)S(1)}, f32[3072,128]{0,1:T(8,128)}, u32[]{:S(2)}, u32[]{:S(2)}) collective-permute-start(f32[3072,128]{0,1:T(8,128)S(1)} %bitcast.149), channel_id=1, source_target_pairs={{0,12},{4,0},{8,4},{12,8},{1,13},{5,1},{9,5},{13,9},{2,14},{6,2},{... | collective-permute-start | bytes 4718600 | tf_op jit(solution)/shard_map/ppermute | solution.py:22
  422.7 22.1 %copy-start.9 = (f32[1,2,256]{2,1,0:T(2,128)S(1)}, f32[1,2,256]{2,1,0:T(2,128)}, u32[]{:S(2)}) copy-start(f32[1,2,256]{2,1,0:T(2,128)} %param.19) | copy-start | bytes 6148
  422.8 57.7 %copy-start.2 = (f32[12288,128]{1,0:T(8,128)}, f32[12288,128]{1,0:T(8,128)S(1)}, u32[]{:S(2)}) copy-start(f32[12288,128]{1,0:T(8,128)S(1)} %constant_dynamic-update-slice_fusion.3) | copy-start | bytes 18874372
  480.5 44.2 %collective-permute-start.5 = (f32[3072,128]{0,1:T(8,128)}, f32[3072,128]{0,1:T(8,128)}, u32[]{:S(2)}, u32[]{:S(2)}) collective-permute-start(f32[3072,128]{0,1:T(8,128)} %collective-permute-done.3), channel_id=1, source_target_pairs={{0,4},{4,8},{8,12},{12,0},{1,5},{5,9},{9,13},{13,1},{2,6},{6,10},{... | collective-permute-start | bytes 4718600 | tf_op jit(solution)/shard_map/ppermute | solution.py:19
  480.7 4.3 collective-permute-start.9
  482.6 32.8 %collective-permute-start.8 = (f32[1,4]{1,0:T(1,128)S(1)}, f32[1,4]{1,0:T(1,128)S(1)}, u32[]{:S(2)}, u32[]{:S(2)}) collective-permute-start(f32[1,4]{1,0:T(1,128)S(1)} %pad_maximum_fusion.2), channel_id=1, source_target_pairs={{0,1},{1,2},{2,3},{3,4},{4,5},{5,6},{6,7},{7,8},{8,9},{9,10},{10,1... | collective-permute-start | bytes 56 | tf_op jit(solution)/shard_map/ppermute | solution.py:42
  566.0 43.3 %copy-start.1 = (f32[1,256,256]{2,1,0:T(8,128)S(1)}, f32[1,256,256]{2,1,0:T(8,128)}, u32[]{:S(2)}) copy-start(f32[1,256,256]{2,1,0:T(8,128)} %param.18) | copy-start | bytes 786436
  (3 other events, 3.4 us)
Sparse Core Ops, SparseCore 0:
  43.0 43.9 all-reduce.4
  91.1 33.7 all-reduce.6
  305.3 43.0 all-reduce.8
  352.5 33.7 all-reduce.10
